TPU v7x, 256 devices: a whole 4x4x8 slice. The times are simulated.
256 devices in a mesh: grp: 8 (over z_lo, y), tile: 32 (over x, z_hi, core).
Axes of the slice: x: 4, y: 4, z: 8 (z_hi: 4, z_lo: 2; z = z_hi * 2 + z_lo), core: 2. Of those that a mesh axis runs over, the one named last changes fastest.
Arguments:
- latent: bfloat16 [256, 2, 32, 32, 512], P(('grp', 'tile')), parts along dimension 0
- lengths: int32 [16], P('grp'), parts along dimension 0, may hold values from 1 to 2, as said below
- tile_of_slot: int32 [256], P('grp'), parts along dimension 0, may hold values from 0 to 31, each once
- norm_gain: float32 [512], replicated, may hold values from 0.5 to 1.5
- norm_shift: float32 [512], replicated, may hold values from -3 to 3
- conv_weight: bfloat16 [3, 3, 3, 512, 256], replicated, may hold values from -0.0546875 to 0.0546875
- conv_bias: float32 [256], replicated, may hold values from -3 to 3
Outputs:
- decoded: bfloat16 [256, 2, 32, 32, 256], P(('grp', 'tile')), parts along dimension 0
There are 8 independent parts, one for each index of `grp`. A program takes and returns all parts, laid end to end along the dimension named above; an argument that names none is the same for every part. Nothing has to cross between parts.
Inputs may be any that keep to these rules, and one draw needn't show every extreme that they name: `lengths`: one of the two videos has all 2 frames, the other fewer.
All inputs are finite; a program needn't handle non-finite values.
Results may differ from a plain program's by a relative error of at most 0.0044.
Values may be sent and summed in bfloat16 or wider, within the bound.
A program may use at most 128 MiB of HBM per device.

v0:
```python
import jax
import jax.numpy as jnp
from jax import lax
from jax.sharding import PartitionSpec as P

GROUPS = 32
TX = 4


def normalize(values, chan_mean, chan_inv, norm_gain, norm_shift):
    normed = (values.astype(jnp.float32) - chan_mean) * chan_inv * norm_gain + norm_shift
    return jax.nn.silu(normed).astype(jnp.bfloat16)


def body(latent, lengths, tile_of_slot, norm_gain, norm_shift, conv_weight, conv_bias):
    tiles = lax.axis_size("tile")
    across = TX
    down_count = tiles // (2 * across)
    per_video = down_count * across
    my_slot = lax.axis_index("tile")
    my_tile = tile_of_slot[my_slot]
    my_video = my_tile // per_video
    tile_row = my_tile % per_video // across
    tile_col = my_tile % across
    frames = latent.shape[1]
    rows_here = latent.shape[2]
    cols_here = latent.shape[3]
    channels = latent.shape[4]
    outputs = conv_weight.shape[4]
    groups_size = channels // GROUPS
    own = latent[0]
    values = own.astype(jnp.float32)
    my_length = lengths[my_video]
    frame_mask = (jnp.arange(frames, dtype=jnp.int32) < my_length).astype(jnp.float32)
    masked = values * frame_mask[:, None, None, None]
    local_sum = jnp.sum(masked, axis=(0, 1, 2))
    local_square = jnp.sum(masked * values, axis=(0, 1, 2))
    pick = (jnp.arange(2, dtype=jnp.int32) == my_video).astype(jnp.float32)
    terms = pick[:, None, None] * jnp.stack([local_sum, local_square])[None]
    totals = lax.psum(terms, "tile")
    grouped = totals.reshape(2, 2, GROUPS, groups_size).sum(-1)
    count = (
        lengths.astype(jnp.float32)
        * float(down_count * rows_here * across * cols_here * groups_size)
    )[:, None]
    mean = grouped[:, 0] / count
    inv = 1.0 / jnp.sqrt(grouped[:, 1] / count - mean * mean + 1e-06)
    chan_mean = jnp.repeat(mean, groups_size, axis=1)[my_video]
    chan_inv = jnp.repeat(inv, groups_size, axis=1)[my_video]
    hidden = normalize(own, chan_mean, chan_inv, norm_gain, norm_shift)
    stacked = hidden[None]
    gathered = (
        lax.all_gather(stacked[:, :, :1], "tile", axis=0, tiled=True),
        lax.all_gather(stacked[:, :, -1:], "tile", axis=0, tiled=True),
        lax.all_gather(stacked[:, :, :, :1], "tile", axis=0, tiled=True),
        lax.all_gather(stacked[:, :, :, -1:], "tile", axis=0, tiled=True),
    )
    finish = lambda piece: piece
    top_rows, bottom_rows, left_cols, right_cols = gathered
    slot_range = jnp.arange(tiles, dtype=jnp.int32)

    def fetch(source, row_step, col_step):
        near_row = tile_row + row_step
        near_col = tile_col + col_step
        inside = (near_row >= 0) & (near_row < down_count) & (near_col >= 0) & (near_col < across)
        neighbour = (
            my_video * per_video
            + jnp.clip(near_row, 0, down_count - 1) * across
            + jnp.clip(near_col, 0, across - 1)
        )
        found = jnp.sum(jnp.where(tile_of_slot == neighbour, slot_range, 0))
        piece = lax.dynamic_index_in_dim(source, found, 0, keepdims=False)
        return finish(piece) * inside.astype(jnp.bfloat16)

    upper = fetch(bottom_rows, -1, 0)[:, 0]
    lower = fetch(top_rows, 1, 0)[:, 0]
    left_side = fetch(right_cols, 0, -1)[:, :, 0]
    right_side = fetch(left_cols, 0, 1)[:, :, 0]
    upper_left = fetch(bottom_rows, -1, -1)[:, 0, -1]
    upper_right = fetch(bottom_rows, -1, 1)[:, 0, 0]
    lower_left = fetch(top_rows, 1, -1)[:, 0, -1]
    lower_right = fetch(top_rows, 1, 1)[:, 0, 0]
    middle = jnp.concatenate([left_side[:, :, None], hidden, right_side[:, :, None]], axis=2)
    top_line = jnp.concatenate([upper_left[:, None], upper, upper_right[:, None]], axis=1)
    bottom_line = jnp.concatenate([lower_left[:, None], lower, lower_right[:, None]], axis=1)
    padded = jnp.concatenate([top_line[:, None], middle, bottom_line[:, None]], axis=1)
    padded = jnp.concatenate([padded[:1], padded[:1], padded], axis=0)
    total = jnp.zeros((frames * rows_here * cols_here, outputs), jnp.float32)
    for depth in range(3):
        for row_off in range(3):
            for col_off in range(3):
                window = padded[
                    depth : depth + frames,
                    row_off : row_off + rows_here,
                    col_off : col_off + cols_here,
                ].reshape(-1, channels)
                total = total + jnp.dot(
                    window, conv_weight[depth, row_off, col_off], preferred_element_type=jnp.float32
                )
    conv = total.reshape(frames, rows_here, cols_here, outputs) + conv_bias
    conv = conv * frame_mask[:, None, None, None]
    return conv.astype(jnp.bfloat16)[None]


def solution(mesh):
    placed = (P(("grp", "tile"), None, None, None, None), P("grp"), P("grp"), P(), P(), P(), P())
    return jax.shard_map(
        body,
        mesh=mesh,
        in_specs=placed,
        out_specs=P(("grp", "tile"), None, None, None, None),
        check_vma=False,
    )
```

profile of v0, /device:TPU:1, one launch (start us, length us, event | category | flops | bytes accessed | tf_op | source)
XLA Modules:
  0.0 457.6 jit_solution(8964397415507494311)
XLA Ops:
  6.5 1.4 dynamic_slice.38
  11.2 1.2 dynamic_slice.39
  13.1 2.6 multiply_reduce_fusion
  15.9 141.0 %psum.7 = f32[2,2,32,16]{3,2,1,0:T(8,128)S(1)} all-reduce(f32[2,2,32,16]{3,2,1,0:T(8,128)S(1)} %reshape.242), channel_id=1, replica_groups=mesh['grp'=8,'tile'=32] {'tile'}, use_global_device_ids=true, to_apply=%region_2.3 | all-reduce | flops 2048 | bytes 16384 | tf_op jit(solution)/shard_map/psum | solution.py:40
  157.5 1.4 fusion.18
  158.9 1.3 copy-done.3
  161.2 1.5 fusion.95
  164.3 0.8 fusion.86
  181.2 3.0 fusion.9
  184.2 32.4 %all-gather.9.cloned.1.call-done = bf16[32,2,32,1,512]{4,2,3,1,0:T(8,128)(2,1)} async-done(((bf16[1,2,32,1,512]{4,2,3,1,0:T(8,128)(2,1)}), bf16[32,2,32,1,512]{4,2,3,1,0:T(8,128)(2,1)}) %all-gather.9.cloned.1.call-update) | async-done | bytes 2097168 | tf_op jit(solution)/shard_map/all_gather | solution.py:55
  216.6 0.8 multiply_bitcast_fusion.3
  217.6 53.3 %all-gather.11.cloned.1.call-done = bf16[32,2,1,32,512]{4,3,2,1,0:T(8,128)(2,1)} async-done(((bf16[1,2,1,32,512]{4,3,2,1,0:T(8,128)(2,1)}), bf16[32,2,1,32,512]{4,3,2,1,0:T(8,128)(2,1)}) %all-gather.11.cloned.1.call-update) | async-done | bytes 2097168 | tf_op jit(solution)/shard_map/all_gather | solution.py:53
  270.9 0.9 multiply_bitcast_fusion.1
  271.8 53.4 %all-gather.5.cloned.1.call-done = bf16[32,2,1,32,512]{4,3,2,1,0:T(8,128)(2,1)} async-done(((bf16[1,2,1,32,512]{4,3,2,1,0:T(8,128)(2,1)}), bf16[32,2,1,32,512]{4,3,2,1,0:T(8,128)(2,1)}) %all-gather.5.cloned.1.call-update) | async-done | bytes 2097168 | tf_op jit(solution)/shard_map/all_gather | solution.py:54
  325.2 0.9 multiply_bitcast_fusion.6
  326.1 0.9 multiply_bitcast_fusion.2
  326.9 0.8 multiply_bitcast_fusion.7
  327.8 51.5 %all-gather.7.cloned.1.call-done = bf16[32,2,32,1,512]{4,2,3,1,0:T(8,128)(2,1)} async-done(((bf16[1,2,32,1,512]{4,2,3,1,0:T(8,128)(2,1)}), bf16[32,2,32,1,512]{4,2,3,1,0:T(8,128)(2,1)}) %all-gather.7.cloned.1.call-update) | async-done | bytes 2097168 | tf_op jit(solution)/shard_map/all_gather | solution.py:56
  379.3 0.8 multiply_bitcast_fusion.4
  380.3 0.8 pad_maximum_fusion.4
  381.1 8.4 %pad_maximum_fusion.3 = (bf16[2,32,32,512]{3,2,1,0:T(8,128)(2,1)}, bf16[2,32,32,512]{3,2,1,0:T(8,128)(2,1)}, bf16[2,32,32,512]{3,2,1,0:T(8,128)(2,1)}, bf16[2,32...) fusion(bf16[1,34,34,512]{3,2,1,0:T(8,128)(2,1)S(1)} %pad_maximu, ...), kind=kLoop, calls=%fused_computation.79 | loop fusion | flops 37748736 | bytes 20058112 | tf_op jit(solution)/shard_map/concatenate | solution.py:87
  389.5 2.1 maximum_maximum_fusion
  391.6 4.5 pad_maximum_fusion
  396.1 4.7 %pad_maximum_fusion.1 = (bf16[2,32,32,512]{3,2,1,0:T(8,128)(2,1)}, bf16[2,32,32,512]{3,2,1,0:T(8,128)(2,1)}) fusion(bf16[2,32,1,512]{3,2,1,0:T(2,128)(2,1)S(1)} %copy.117, bf16[2,32,32,512]{3,2,1,0:T(8,128)(2,1)S(1)} %fusion.9, bf16[2,32,1,512]{3,2,1,0:T(2,128)(2,1)S(1)} %copy.116), kind=kLoop, calls=%fused_computation.77 | loop fusion | flops 8388608 | bytes 6422528 | tf_op jit(solution)/shard_map/concatenate | solution.py:83
  400.7 8.5 %fusion.91 = (bf16[2,32,32,512]{3,2,1,0:T(8,128)(2,1)S(1)}, bf16[2,32,32,512]{3,2,1,0:T(8,128)(2,1)}, bf16[2,32,32,512]{3,2,1,0:T(8,128)(2,1)}, bf16[2,32,32,512...) fusion(bf16[3,34,34,512]{3,2,1,0:T(8,128)(2,1)S(1)} %maximum_ma, ...), kind=kLoop, calls=%fused_computation.180 | loop fusion | bytes 37748736 | tf_op jit(solution)/shard_map/slice | solution.py:92
  409.2 1.5 fusion.93
  410.8 1.5 fusion.92
  412.4 1.8 fusion.54
  414.2 1.8 convolution_add_fusion.25
  416.1 1.8 convolution_add_fusion.24
  418.6 0.9 copy-done.17
  420.2 0.9 copy-done.15
  421.1 0.7 convolution_add_fusion.21
  421.8 0.9 copy-done.13
  422.7 0.7 convolution_add_fusion.20
  423.4 0.9 copy-done.11
  424.3 0.7 convolution_add_fusion.19
  425.0 0.9 copy-done.9
  425.9 0.7 convolution_add_fusion.18
  426.6 0.9 copy-done.20
  427.5 0.7 convolution_add_fusion.17
  428.2 0.9 copy-done.18
  429.1 0.7 convolution_add_fusion.16
  429.8 0.9 copy-done.16
  430.7 0.7 convolution_add_fusion.15
  431.4 0.9 copy-done.14
  432.3 0.7 convolution_add_fusion.14
  433.0 0.9 copy-done.12
  433.8 0.9 convolution_add_fusion.13
  436.1 0.9 copy-done.8
  437.7 0.9 copy-done.7
  439.3 0.7 convolution_add_fusion.9
  440.1 0.7 convolution_add_fusion.8
  440.8 0.7 convolution_add_fusion.7
  441.5 0.7 convolution_add_fusion.6
  442.3 0.8 copy-done.6
  443.1 0.7 convolution_add_fusion.5
  443.8 0.9 copy-done.4
  444.7 0.7 convolution_add_fusion.4
  445.4 0.9 copy-done.5
  447.0 0.7 convolution_add_fusion.2
  447.8 0.7 convolution_add_fusion.1
  448.5 0.7 convolution_add_fusion
  449.2 1.6 multiply_convert_fusion
  (82 shorter events, 9.6 us)
Async XLA Ops:
  6.5 150.9 %copy-start.1 = (bf16[1,2,32,32,512]{4,3,2,1,0:T(8,128)(2,1)S(1)}, bf16[1,2,32,32,512]{4,3,2,1,0:T(8,128)(2,1)}, u32[]{:S(2)}) copy-start(bf16[1,2,32,32,512]{4,3,2,1,0:T(8,128)(2,1)} %param.7) | copy-start | bytes 6291460
  6.5 150.9 %copy-start.23 = (f32[512]{0:T(512)S(1)}, f32[512]{0:T(512)}, u32[]{:S(2)}) copy-start(f32[512]{0:T(512)} %param.11) | copy-start | bytes 6148
  6.5 150.9 %copy-start.24 = (f32[512]{0:T(512)S(1)}, f32[512]{0:T(512)}, u32[]{:S(2)}) copy-start(f32[512]{0:T(512)} %param.10) | copy-start | bytes 6148
  6.5 210.1 %all-gather.9.cloned.1.call-start = ((), (), s32[]{:S(2)}) async-start(), calls=%async_computation.2 | async-start | bytes 2162688 | tf_op jit(solution)/shard_map/all_gather | solution.py:55
  157.5 6.8 %copy-start.26 = (s32[32]{0:T(128)S(1)}, s32[32]{0:T(128)}, u32[]{:S(2)}) copy-start(s32[32]{0:T(128)} %param.9) | copy-start | bytes 388
  158.9 1.4 copy-start.3
  161.2 109.7 %all-gather.11.cloned.1.call-start = ((), (), s32[]{:S(2)}) async-start(), calls=%async_computation.3 | async-start | bytes 2162688 | tf_op jit(solution)/shard_map/all_gather | solution.py:53
  162.8 162.4 %all-gather.5.cloned.1.call-start = ((), (), s32[]{:S(2)}) async-start(), calls=%async_computation | async-start | bytes 2162688 | tf_op jit(solution)/shard_map/all_gather | solution.py:54
  163.5 215.8 %all-gather.7.cloned.1.call-start = ((), (), s32[]{:S(2)}) async-start(), calls=%async_computation.1 | async-start | bytes 2162688 | tf_op jit(solution)/shard_map/all_gather | solution.py:56
  400.7 8.5 %copy-start = (bf16[2,33,34,512]{3,2,1,0:T(8,128)(2,1)S(1)}, bf16[2,33,34,512]{3,2,1,0:T(8,128)(2,1)}, u32[]{:S(2)}) copy-start(bf16[2,33,34,512]{3,2,1,0:T(8,128)(2,1)} %get-tuple-element.33) | copy-start | bytes 6893572
  410.8 1.6 copy-start.2
  412.4 1.8 copy-start.22
  412.4 5.5 %slice-start = ((s8[7077888]{0:T(1024)(128)(4,1)}), s8[4194304]{0:T(1024)(128)(4,1)S(1)}, s32[]{:S(2)}) async-start(s8[7077888]{0:T(1024)(128)(4,1)} %bitcast.242), calls=%async_computation.4 | async-start | bytes 8388608
  414.2 1.9 copy-start.21
  414.2 3.7 slice-start.1
  416.1 1.9 copy-start.19
  417.9 1.6 copy-start.17
  419.5 1.6 copy-start.15
  421.1 1.6 copy-start.13
  422.7 1.6 copy-start.11
  424.3 1.6 copy-start.9
  425.9 1.6 copy-start.20
  427.5 1.6 copy-start.18
  429.1 1.6 copy-start.16
  430.7 1.6 copy-start.14
  432.3 1.6 copy-start.12
  433.8 1.6 copy-start.10
  435.4 1.6 copy-start.8
  437.0 1.6 copy-start.7
  441.5 1.6 copy-start.6
  443.1 1.6 copy-start.4
  444.7 1.6 copy-start.5
  448.5 0.8 copy-start.25
Sparse Core Ops, SparseCore 0:
  161.3 55.3 all-gather.8
  219.2 51.6 all-gather.10
  273.5 51.6 all-gather.4
  327.6 51.6 all-gather.6
where the time goes:
time: 464 us; the launch traced here: 458 us
  waiting for transfers between devices  191 us (41%)
  blocking collectives  141 us (30%)
  other arithmetic  36.7 us (8%)
  local copies, waits for them, and re-layouts  33.1 us (7%)
  between operations  32.6 us (7%)
  matrix products  22.7 us (5%)
    psum x1, blocking collectives, body(): totals = lax.psum(terms, 'tile')  141 us
    all_gather x1, waiting for transfers between devices, body(): lax.all_gather(stacked[:, :, -1:], 'tile', axis=0, tiled=True)  53.4 us
    all_gather x1, waiting for transfers between devices, body(): lax.all_gather(stacked[:, :, :1], 'tile', axis=0, tiled=True)  53.3 us
    all_gather x1, waiting for transfers between devices, body(): lax.all_gather(stacked[:, :, :, -1:], 'tile', axis=0, tiled=True)  51.5 us
    all_gather x1, waiting for transfers between devices, body(): lax.all_gather(stacked[:, :, :, :1], 'tile', axis=0, tiled=True)  32.4 us
    dot_general x27, matrix products, body(): jnp.dot(window, conv_weight[depth, row_off, col_off], preferred_element_t...  22.7 us
    unnamed x58, local copies, waits for them, and re-layouts  15.2 us
    slice x3, local copies, waits for them, and re-layouts, body(): padded[depth:depth + frames, row_off:row_off + rows_here, col_off:col_off...  11.6 us
  transfers between devices with their start and end apart: 4, of which 4 were waited for; matrix products, arithmetic and copies ran while one was open for 2% of the time, Pallas kernels for 0%

commit v1 on v0

v1 whole, which is shorter than its diff:
```python
import functools

import jax
import jax.numpy as jnp
from jax import lax
from jax.experimental import pallas as pl
from jax.experimental.pallas import tpu as pltpu
from jax.sharding import PartitionSpec as P

MESH = pl.DeviceIdType.MESH
F32 = jnp.float32
BF16 = jnp.bfloat16
GROUPS = 32
N = 32
ROWS = 32
COLS = 32
C = 512
CO = 256
CG = C // GROUPS
PER_VIDEO = 16
TX = 4
TY = 4
COUNT = float(TY * ROWS * TX * COLS * CG)
CHUNK = 8


def iota(shape, dim):
    return lax.broadcasted_iota(jnp.int32, shape, dim)


def exact_dot(a, b):
    return jnp.dot(a, b, precision=lax.Precision.HIGHEST, preferred_element_type=F32)


def dot(a, b):
    return jnp.dot(a, b, preferred_element_type=F32)


def activate(x, mean, scale, shift):
    y = (x - mean) * scale + shift
    half = 0.5 * y
    return (half + half * jnp.tanh(half)).astype(BF16).astype(F32)


def kernel(
    lat_hbm, w_hbm, tos_s, len_s, tos_v, gain_ref, shift_ref, bias_ref, out_ref,
    lat, w, wa, hp, acc, send1, recv1, send2, recv2, stat, srecv, norm, edge, pick,
    lat_sem, w_sem, ssem, rsem,
):
    me = lax.axis_index("tile")
    grp = lax.axis_index("grp")

    def other(k):
        return lax.rem(me + k, N)

    barrier = pltpu.get_barrier_semaphore()

    def greet(k, carry):
        pl.semaphore_signal(barrier, inc=1, device_id=(grp, other(k)), device_id_type=MESH)
        return carry

    lax.fori_loop(1, N, greet, 0)
    lat_copy = pltpu.make_async_copy(lat_hbm, lat, lat_sem)
    lat_copy.start()
    w_copy = pltpu.make_async_copy(w_hbm, w, w_sem)
    w_copy.start()

    def send(phase, src, dst, by_target):
        def one(k, carry):
            to = other(k)
            pltpu.make_async_remote_copy(
                src_ref=src.at[to] if by_target else src,
                dst_ref=dst.at[me],
                send_sem=ssem.at[phase],
                recv_sem=rsem.at[phase],
                device_id=(grp, to),
                device_id_type=MESH,
            ).start()
            return carry

        lax.fori_loop(1, N, one, 0)

    def whole(phase, dst):
        part = dst.at[pl.ds(0, N - 1)]
        return pltpu.make_async_remote_copy(
            src_ref=part, dst_ref=part, send_sem=ssem.at[phase], recv_sem=rsem.at[phase],
            device_id=(grp, other(1)), device_id_type=MESH,
        )

    my_tile = tos_s[me]
    my_second = my_tile >= PER_VIDEO
    my_length = jnp.where(my_second, len_s[1], len_s[0])
    valid = [jnp.where(my_length > f, 1.0, 0.0).astype(F32) for f in range(2)]

    lat_copy.wait()
    total = jnp.zeros((1, C), F32)
    squares = jnp.zeros((1, C), F32)
    for f in range(2):

        def row_sums(r, carry):
            s, q = carry
            x = lat[f, r].astype(F32)
            return s + x, q + x * x

        zero = jnp.zeros((COLS, C), F32)
        s, q = lax.fori_loop(0, ROWS, row_sums, (zero, zero))
        total = total + valid[f] * jnp.sum(s, axis=0, keepdims=True)
        squares = squares + valid[f] * jnp.sum(q, axis=0, keepdims=True)
    chan, lane = iota((C, 128), 0), iota((C, 128), 1)
    to_sum = jnp.where(chan // CG == lane, 1.0, 0.0).astype(F32)
    to_square = jnp.where(chan // CG + GROUPS == lane, 1.0, 0.0).astype(F32)
    packed = exact_dot(jnp.broadcast_to(total, (8, C)), to_sum) + exact_dot(
        jnp.broadcast_to(squares, (8, C)), to_square
    )
    stat[...] = packed[0:1]

    sub = iota((8, C), 0)

    def edge_rows(f, e, p):
        if e < 2:
            return lat[f, 0 if e == 0 else ROWS - 1, 8 * p : 8 * p + 8].astype(F32)
        found = jnp.zeros((8, C), F32)
        for q in range(8):
            if e == 2:
                block = lat[f, 8 * p + q, 0:16].astype(F32)[0:8]
                turned = pltpu.roll(block, q, 0) if q else block
            else:
                block = lat[f, 8 * p + q, 16:32].astype(F32)[8:16]
                turned = pltpu.roll(block, q + 1, 0) if q < 7 else block
            found = jnp.where(sub == q, turned, found)
        return found

    def fold(x):
        return jnp.concatenate([x[:, : C // 2], x[:, C // 2 :]], axis=0).astype(BF16)

    for e in range(4):
        for p in range(4):
            first, second = edge_rows(0, e, p), edge_rows(1, e, p)
            send1[e * 8 + 2 * p] = fold(jnp.where(sub < 4, first, pltpu.roll(second, 4, 0)))
            send1[e * 8 + 2 * p + 1] = fold(jnp.where(sub < 4, pltpu.roll(first, 4, 0), second))

    pl.semaphore_wait(barrier, N - 1)
    send(0, stat, srecv, False)
    send(1, send1, recv1, True)
    srecv[me] = stat[...]
    recv1[me] = send1[me]

    kind = me // 8
    part = lax.rem(me, 8)
    tos_row = tos_v[...].astype(F32)
    owner = iota((N * 8, N), 0) // 8
    tile_here = jnp.sum(
        jnp.where(owner == iota((N * 8, N), 1), jnp.broadcast_to(tos_row, (N * 8, N)), 0.0),
        axis=1, keepdims=True,
    ).astype(jnp.int32)
    expand = jnp.where(iota((N, N * 8), 0) == iota((N, N * 8), 1) // 8, 1.0, 0.0).astype(F32)
    tile_there = exact_dot(jnp.broadcast_to(tos_row, (8, N)), expand)[0:1].astype(jnp.int32)
    row_step = jnp.where(kind == 0, 1, jnp.where(kind == 1, -1, 0))
    col_step = jnp.where(kind == 2, 1, jnp.where(kind == 3, -1, 0))
    px = lax.rem(iota((N * 8, 1), 0), 4)
    same_row = lax.rem(iota((N * 8, N * 8), 0), 8) == lax.rem(iota((N * 8, N * 8), 1), 8)
    video = tile_here // PER_VIDEO
    tile_row = lax.rem(tile_here, PER_VIDEO) // TX
    tile_col = lax.rem(tile_here, TX)
    low_end = jnp.where((px == 0) & (part == 0), 1, 0)
    high_end = jnp.where((px == 3) & (part == 7), 1, 0)
    for side in range(2):
        near_row = tile_row + row_step
        near_col = tile_col + col_step
        if side == 1:
            turn = jnp.where(kind < 2, 1, 100)
            near_col = near_col + turn * low_end - turn * high_end
        inside = (near_row >= 0) & (near_row < TY) & (near_col >= 0) & (near_col < TX)
        near = jnp.where(inside, video * PER_VIDEO + near_row * TX + near_col, -1)
        pick[side] = jnp.where((near == tile_there) & same_row, 1.0, 0.0).astype(BF16)

    w_copy.wait()

    def add_weights(i, carry):
        tap, at = i // 4, pl.multiple_of(lax.rem(i, 4) * 128, 128)
        rows = pl.ds(at, 128)
        whole_sum = (
            w[tap, rows].astype(F32) + w[9 + tap, rows].astype(F32) + w[18 + tap, rows].astype(F32)
        )
        wa[tap, rows] = whole_sum.astype(BF16)
        return carry

    lax.fori_loop(0, 36, add_weights, 0)
    for u in range(2):
        hp[u, 0] = jnp.zeros((COLS, C), BF16)
        hp[u, ROWS + 1] = jnp.zeros((COLS, C), BF16)

    whole(0, srecv).wait_recv()
    sums = [jnp.zeros((1, 128), F32), jnp.zeros((1, 128), F32)]
    for s in range(N):
        row = srecv[s]
        second = jnp.where(tos_s[s] >= PER_VIDEO, 1.0, 0.0).astype(F32)
        sums = [sums[0] + row * (1.0 - second), sums[1] + row * second]
    lane, chan = iota((128, C), 0), iota((128, C), 1)
    from_sum = jnp.where(chan // CG == lane, 1.0, 0.0).astype(F32)
    from_square = jnp.where(chan // CG + GROUPS == lane, 1.0, 0.0).astype(F32)
    for v in range(2):
        count = len_s[v].astype(F32) * COUNT
        spread = jnp.broadcast_to(sums[v], (8, 128))
        mean = exact_dot(spread, from_sum) / count
        square = exact_dot(spread, from_square) / count
        norm[v, 0] = mean
        norm[v, 1] = (1.0 / jnp.sqrt(square - mean * mean + 1e-06)) * gain_ref[...]
    shift8 = jnp.broadcast_to(shift_ref[...], (8, C))

    def halves(x):
        return jnp.concatenate([x[:, : C // 2], x[:, C // 2 :]], axis=0)

    shift16 = halves(shift8)
    half_sub = iota((8, C // 2), 0)
    whole(1, recv1).wait_recv()

    def chunk_rows(p, carry):
        parts = [[], []]
        for j in range(2):
            s = 2 * p + j
            v = jnp.where(tos_s[s] >= PER_VIDEO, 1, 0)
            h = activate(recv1[s].astype(F32), halves(norm[v, 0]), halves(norm[v, 1]), shift16)
            for half in range(2):
                x = h[8 * half : 8 * half + 8]
                parts[half].append(jnp.where(half_sub < 4, x, x - pltpu.roll(x, 4, 0)))
        for half in range(2):
            edge[half, pl.ds(pl.multiple_of(16 * p, 16), 16)] = jnp.concatenate(
                parts[half], axis=0
            ).astype(BF16)
        return carry

    lax.fori_loop(0, N // 2, chunk_rows, 0)
    base = jnp.where(kind == 0, 6, jnp.where(kind == 2, 2, 0))
    stride = jnp.where(kind < 2, 1, 3)
    row8 = lax.rem(iota((N * 8, CO), 0), 8)
    px = lax.rem(row8, 4)
    half_c = C // 2
    taps = []
    for t in range(3):
        tap = base + stride * t
        ya = dot(edge[0], wa[tap, :half_c]) + dot(edge[1], wa[tap, half_c:])
        yc = dot(edge[0], w[18 + tap, :half_c]) + dot(edge[1], w[18 + tap, half_c:])
        taps.append(jnp.where(row8 < 4, ya, yc))
    main = (
        taps[1]
        + jnp.where(px >= 1, pltpu.roll(taps[0], 1, 0), 0.0)
        + jnp.where(px <= 2, pltpu.roll(taps[2], N * 8 - 1, 0), 0.0)
    )
    extra = jnp.where(px == 3, taps[0], jnp.where(px == 0, taps[2], 0.0))
    main = dot(pick[0], main.astype(BF16)).reshape(N, 8, CO)
    extra = dot(pick[1], extra.astype(BF16)).reshape(N, 8, CO)
    send2[...] = jnp.concatenate([main, extra], axis=1).astype(BF16)
    send(2, send2, recv2, True)
    recv2[me] = send2[me]

    mine = jnp.where(my_second, 1, 0)
    mean = jnp.concatenate([norm[mine, 0]] * 4, axis=0)
    scale = jnp.concatenate([norm[mine, 1]] * 4, axis=0)
    shift = jnp.concatenate([shift8] * 4, axis=0)

    def hidden_row(r, carry):
        first = activate(lat[0, r].astype(F32), mean, scale, shift)
        second = activate(lat[1, r].astype(F32), mean, scale, shift)
        hp[0, r + 1] = first.astype(BF16)
        hp[1, r + 1] = (second - first).astype(BF16)
        return carry

    lax.fori_loop(0, ROWS, hidden_row, 0)
    col = lax.rem(iota((CHUNK * COLS, CO), 0), COLS)
    for u in range(2):

        def conv_rows(i, carry):
            r0 = i * CHUNK
            parts = []
            for c in range(3):
                part_sum = None
                for b in range(3):
                    window = hp[u, pl.ds(r0 + b, CHUNK)].reshape(CHUNK * COLS, C)
                    weight = wa[3 * b + c] if u == 0 else w[18 + 3 * b + c]
                    product = dot(window, weight)
                    part_sum = product if part_sum is None else part_sum + product
                parts.append(part_sum)
            result = (
                parts[1]
                + jnp.where(col > 0, pltpu.roll(parts[0], 1, 0), 0.0)
                + jnp.where(col < COLS - 1, pltpu.roll(parts[2], CHUNK * COLS - 1, 0), 0.0)
            )
            acc[u, pl.ds(r0, CHUNK)] = result.reshape(CHUNK, COLS, CO)
            return carry

        lax.fori_loop(0, ROWS // CHUNK, conv_rows, 0)

    whole(2, recv2).wait_recv()

    def hits(shape, unit, pos):
        at = iota(shape, 1)
        g, r = at // 16, lax.rem(at, 16)
        from_px = lax.rem(r, 4)
        lands = jnp.where(
            r < 8,
            4 * g + from_px,
            jnp.where(
                from_px == 0,
                lax.rem(4 * g + 31, 32),
                jnp.where(from_px == 3, lax.rem(4 * g + 4, 32), -1),
            ),
        )
        return (lax.rem(r, 8) // 4 == unit) & (lands == pos)

    line_at = iota((64, 128), 0)
    to_line = jnp.where(hits((64, 128), line_at // 32, lax.rem(line_at, 32)), 1.0, 0.0).astype(BF16)
    for e, row in ((0, ROWS - 1), (1, 0)):
        line = dot(to_line, recv2[8 * e : 8 * e + 8].reshape(128, CO))
        acc[0, row] += line[:COLS]
        acc[1, row] += line[COLS:]
    side_at = iota((512, 128), 0)
    on_side = hits((512, 128), side_at // 256, lax.rem(side_at, 256) // 8)
    for e, at in ((2, COLS - 8), (3, 0)):
        to_side = jnp.where(on_side & (lax.rem(side_at, 8) == (7 if e == 2 else 0)), 1.0, 0.0)
        side = dot(to_side.astype(BF16), recv2[8 * e : 8 * e + 8].reshape(128, CO))
        side = side.reshape(2, ROWS, 8, CO)
        for u in range(2):
            acc[u, :, at : at + 8] += side[u]

    bias = jnp.broadcast_to(bias_ref[...], (COLS, CO))

    def finish(r, carry):
        first = acc[0, r] + bias
        out_ref[0, r] = (first * valid[0]).astype(BF16)
        out_ref[1, r] = ((first + acc[1, r]) * valid[1]).astype(BF16)
        return carry

    lax.fori_loop(0, ROWS, finish, 0)
    whole(0, srecv).wait_send()
    whole(1, recv1).wait_send()
    whole(2, recv2).wait_send()


def body(latent, lengths, tile_of_slot, norm_gain, norm_shift, conv_weight, conv_bias):
    vmem = pl.BlockSpec(memory_space=pltpu.VMEM)
    smem = pl.BlockSpec(memory_space=pltpu.SMEM)
    anywhere = pl.BlockSpec(memory_space=pl.ANY)
    decoded = pl.pallas_call(
        kernel,
        out_shape=jax.ShapeDtypeStruct((2, ROWS, COLS, CO), BF16),
        in_specs=[anywhere, anywhere, smem, smem, vmem, vmem, vmem, vmem],
        out_specs=vmem,
        scratch_shapes=[
            pltpu.VMEM((2, ROWS, COLS, C), BF16),
            pltpu.VMEM((27, C, CO), BF16),
            pltpu.VMEM((9, C, CO), BF16),
            pltpu.VMEM((2, ROWS + 2, COLS, C), BF16),
            pltpu.VMEM((2, ROWS, COLS, CO), F32),
            pltpu.VMEM((N, 16, C // 2), BF16),
            pltpu.VMEM((N, 16, C // 2), BF16),
            pltpu.VMEM((N, 16, CO), BF16),
            pltpu.VMEM((N, 16, CO), BF16),
            pltpu.VMEM((1, 128), F32),
            pltpu.VMEM((N, 1, 128), F32),
            pltpu.VMEM((2, 2, 8, C), F32),
            pltpu.VMEM((2, N * 8, C // 2), BF16),
            pltpu.VMEM((2, N * 8, N * 8), BF16),
            pltpu.SemaphoreType.DMA(()),
            pltpu.SemaphoreType.DMA(()),
            pltpu.SemaphoreType.DMA((3,)),
            pltpu.SemaphoreType.DMA((3,)),
        ],
        compiler_params=pltpu.CompilerParams(
            collective_id=0, has_side_effects=True, vmem_limit_bytes=48 << 20
        ),
    )(
        latent[0],
        conv_weight.reshape(27, C, CO),
        tile_of_slot,
        lengths,
        tile_of_slot.reshape(1, N),
        norm_gain.reshape(1, C),
        norm_shift.reshape(1, C),
        conv_bias.reshape(1, CO),
    )
    return decoded[None]


def solution(mesh):
    placed = (P(("grp", "tile"), None, None, None, None), P("grp"), P("grp"), P(), P(), P(), P())
    return jax.shard_map(
        body,
        mesh=mesh,
        in_specs=placed,
        out_specs=P(("grp", "tile"), None, None, None, None),
        check_vma=False,
    )
```

time: 464 us -> 37.6 us (0.08); the launches traced: 458 us -> 37.4 us
  waiting for transfers between devices: 191 us -> 0 us
  blocking collectives: 141 us -> 0 us
  other arithmetic: 36.7 us -> 0 us
  between operations: 32.6 us -> 0.02 us
  Pallas kernels: 0 us -> 31.5 us
  local copies, waits for them, and re-layouts: 33.1 us -> 5.91 us
  matrix products: 22.7 us -> 0 us
    all_gather x4 -> x0, waiting for transfers between devices: 191 us -> none  [the longest x1 53.4 us: body(): lax.all_gather(stacked[:, :, -1:], 'tile', axis=0, tiled=True)]
    psum x1 -> x0, blocking collectives: 141 us -> none  [body(): totals = lax.psum(terms, 'tile')]
    pallas_call x0 -> x1, Pallas kernels: none -> 31.5 us  [body(): pl.pallas_call(kernel, out_shape=jax.ShapeDtypeStruct((2, ROWS, COLS, CO)...]
    dot_general x27 -> x0, matrix products: 22.7 us -> none  [body(): jnp.dot(window, conv_weight[depth, row_off, col_off], preferred_element_t...]
    concatenate x5 -> x0, other arithmetic: 20.4 us -> none  [the longest x2 10.5 us: body(): padded = jnp.concatenate([padded[:1], padded[:1], padded], axis=0)]
    slice x8 -> x0, local copies, waits for them, and re-layouts: 14.6 us -> none  [the longest x3 11.6 us: body(): padded[depth:depth + frames, row_off:row_off + rows_here, col_off:col_off...]
    unnamed x58 -> x13, local copies, waits for them, and re-layouts: 15.2 us -> 5.91 us
    convert_element_type x5 -> x0, other arithmetic: 6.75 us -> none  [the longest x2 4.48 us: normalize(): return jax.nn.silu(normed).astype(jnp.bfloat16)]
  transfers between devices with their start and end apart: 4 -> 0, of which waited for: 4 -> 0; matrix products, arithmetic and copies ran while one was open for 2% -> 0% of each run, Pallas kernels for 0% -> 0%
where the time goes in v1:
time: 37.6 us; the launch traced here: 37.4 us
  Pallas kernels  31.5 us (84%)
  local copies, waits for them, and re-layouts  5.91 us (16%)
    pallas_call x1, Pallas kernels, body(): pl.pallas_call(kernel, out_shape=jax.ShapeDtypeStruct((2, ROWS, COLS, CO)...  31.5 us
    unnamed x13, local copies, waits for them, and re-layouts  5.91 us

profile of v1, /device:TPU:1, one launch (start us, length us, event | category | flops | bytes accessed | tf_op | source)
XLA Modules:
  0.0 37.4 jit_solution(3397809650232396104)
XLA Ops:
  0.0 0.0 copy-start
  0.0 1.6 %copy-done = bf16[1,2,32,32,512]{4,3,2,1,0:T(8,128)(2,1)S(1)} copy-done((bf16[1,2,32,32,512]{4,3,2,1,0:T(8,128)(2,1)S(1)}, bf16[1,2,32,32,512]{4,3,2,1,0:T(8,128)(2,1)}, u32[]{:S(2)}) %copy-start) | copy-done | bytes 2097176
  1.6 0.0 copy-start.1
  1.6 0.7 %copy-done.1 = s32[32]{0:T(128)S(1)} copy-done((s32[32]{0:T(128)S(1)}, s32[32]{0:T(128)}, u32[]{:S(2)}) %copy-start.1) | copy-done | bytes 152
  2.2 0.0 copy-start.2
  2.2 0.7 %copy-done.2 = f32[512]{0:T(512)S(1)} copy-done((f32[512]{0:T(512)S(1)}, f32[512]{0:T(512)}, u32[]{:S(2)}) %copy-start.2) | copy-done | bytes 2072
  2.9 0.0 copy-start.3
  2.9 0.7 %copy-done.3 = f32[512]{0:T(512)S(1)} copy-done((f32[512]{0:T(512)S(1)}, f32[512]{0:T(512)}, u32[]{:S(2)}) %copy-start.3) | copy-done | bytes 2072
  3.6 0.0 copy-start.4
  3.6 0.7 %copy-done.4 = f32[256]{0:T(256)S(1)} copy-done((f32[256]{0:T(256)S(1)}, f32[256]{0:T(256)}, u32[]{:S(2)}) %copy-start.4) | copy-done | bytes 1048
  4.3 0.0 copy-start.5
  4.3 0.7 %copy-done.5 = s32[2]{0:T(128)S(1)} copy-done((s32[2]{0:T(128)S(1)}, s32[2]{0:T(128)}, u32[]{:S(2)}) %copy-start.5) | copy-done | bytes 32
  4.9 31.5 %shard_map.73 = bf16[2,32,32,256]{3,2,1,0:T(8,128)(2,1)S(1)} custom-call(bf16[2,32,32,512]{3,2,1,0:T(8,128)(2,1)S(1)} %bitcast.8, bf16[27,512,256]{2,1,0:T(8,128)(2,1)} %bitcast.13, s32[32]{0:T(128)S(1)} %copy-done.1, s32[2]{0:T(128)S(1)} %copy-done.5, s32[1,32]{1,0:T(1,128)S(1)} %bitcast.9, f32[1,512]{1,0:T(1,128)S(1)} %bitcast.10, f32[1,512]{1,0:T(1,128)S(1)} %bitcast.11, ...), custom_call_target="tpu_custom_call" | custom-call | tf_op jit(solution)/shard_map/pallas_call | solution.py:344
  36.4 1.0 %copy.9 = bf16[1,2,32,32,256]{4,3,2,1,0:T(8,128)(2,1)} copy(bf16[1,2,32,32,256]{4,3,2,1,0:T(8,128)(2,1)S(1)} %bitcast.7) | data formatting | bytes 2097152
Async XLA Ops:
  0.0 1.6 %copy-start = (bf16[1,2,32,32,512]{4,3,2,1,0:T(8,128)(2,1)S(1)}, bf16[1,2,32,32,512]{4,3,2,1,0:T(8,128)(2,1)}, u32[]{:S(2)}) copy-start(bf16[1,2,32,32,512]{4,3,2,1,0:T(8,128)(2,1)} %param.7) | copy-start | bytes 6291460
  1.6 0.7 %copy-start.1 = (s32[32]{0:T(128)S(1)}, s32[32]{0:T(128)}, u32[]{:S(2)}) copy-start(s32[32]{0:T(128)} %tos_s.1) | copy-start | bytes 388
  2.2 0.7 %copy-start.2 = (f32[512]{0:T(512)S(1)}, f32[512]{0:T(512)}, u32[]{:S(2)}) copy-start(f32[512]{0:T(512)} %param.10) | copy-start | bytes 6148
  2.9 0.7 %copy-start.3 = (f32[512]{0:T(512)S(1)}, f32[512]{0:T(512)}, u32[]{:S(2)}) copy-start(f32[512]{0:T(512)} %param.11) | copy-start | bytes 6148
  3.6 0.7 %copy-start.4 = (f32[256]{0:T(256)S(1)}, f32[256]{0:T(256)}, u32[]{:S(2)}) copy-start(f32[256]{0:T(256)} %param.13) | copy-start | bytes 3076
  4.3 0.7 %copy-start.5 = (s32[2]{0:T(128)S(1)}, s32[2]{0:T(128)}, u32[]{:S(2)}) copy-start(s32[2]{0:T(128)} %len_s.1) | copy-start | bytes 28

commit v2 on v1

v2 whole, which is shorter than its diff:
```python
import functools

import jax
import jax.numpy as jnp
from jax import lax
from jax.experimental import pallas as pl
from jax.experimental.pallas import tpu as pltpu
from jax.sharding import PartitionSpec as P

MESH = pl.DeviceIdType.MESH
F32 = jnp.float32
BF16 = jnp.bfloat16
GROUPS = 32
N = 32
ROWS = 32
COLS = 32
C = 512
CO = 256
CG = C // GROUPS
PER_VIDEO = 16
TX = 4
TY = 4
COUNT = float(TY * ROWS * TX * COLS * CG)
CHUNK = 16
EARLY = 0


def iota(shape, dim):
    return lax.broadcasted_iota(jnp.int32, shape, dim)


def exact_dot(a, b):
    return jnp.dot(a, b, precision=lax.Precision.HIGHEST, preferred_element_type=F32)


def dot(a, b):
    return jnp.dot(a, b, preferred_element_type=F32)


def activate(x, mean, scale, shift):
    y = (x - mean) * scale + shift
    half = 0.5 * y
    return (half + half * jnp.tanh(half)).astype(BF16).astype(F32)


def kernel(
    lat_hbm, w_hbm, tos_hbm, len_hbm, tos_row_hbm, gain_hbm, shift_hbm, bias_hbm, out_ref,
    lat, w, wa, hp, acc, send1, recv1, send2, recv2, stat, srecv, norm, norm16, edge, pick,
    tos_s, len_s, tos_v, gain_ref, shift_ref, bias_ref,
    lat_sem, w_sem, small_sem, ssem, rsem,
):
    me = lax.axis_index("tile")
    grp = lax.axis_index("grp")
    my_x, my_z, my_core = me // 8, lax.rem(me // 2, 4), lax.rem(me, 2)

    def to_all(planes, action, xs=None):
        xs = xs or [lax.rem(my_x + 2 + j, 4) * 8 for j in range(4)]
        cores = [my_core, 1 - my_core]
        for plane in planes:
            for x in xs:
                for core in cores:
                    to = x + plane * 2 + core
                    pl.when(to != me)(functools.partial(action, to))

    by_distance = (
        lax.rem(my_z + 2, 4), 3 - my_z, my_z + 1 - 2 * lax.rem(my_z, 2), my_z
    )
    barrier = pltpu.get_barrier_semaphore()

    def greet(to):
        pl.semaphore_signal(barrier, inc=1, device_id=(grp, to), device_id_type=MESH)

    to_all(by_distance, greet)
    lat_copy = pltpu.make_async_copy(lat_hbm, lat, lat_sem)
    lat_copy.start()
    w_copy = pltpu.make_async_copy(w_hbm, w, w_sem)
    w_copy.start()

    small = [
        pltpu.make_async_copy(src, dst, small_sem.at[i])
        for i, (src, dst) in enumerate(
            (
                (tos_hbm, tos_s), (len_hbm, len_s), (tos_row_hbm, tos_v),
                (gain_hbm, gain_ref), (shift_hbm, shift_ref), (bias_hbm, bias_ref),
            )
        )
    ]
    for copy in small:
        copy.start()

    def send(phase, src, dst, to):
        pltpu.make_async_remote_copy(
            src_ref=src, dst_ref=dst.at[me], send_sem=ssem.at[phase], recv_sem=rsem.at[phase],
            device_id=(grp, to), device_id_type=MESH,
        ).start()

    def whole(phase, dst):
        part = dst.at[pl.ds(0, N - 1)]
        return pltpu.make_async_remote_copy(
            src_ref=part, dst_ref=part, send_sem=ssem.at[phase], recv_sem=rsem.at[phase],
            device_id=(grp, lax.rem(me + 1, N)), device_id_type=MESH,
        )

    for copy in small:
        copy.wait()
    my_tile = tos_s[me]
    my_second = my_tile >= PER_VIDEO
    my_length = jnp.where(my_second, len_s[1], len_s[0])
    valid = [jnp.where(my_length > f, 1.0, 0.0).astype(F32) for f in range(2)]

    lat_copy.wait()
    total = jnp.zeros((1, C), F32)
    squares = jnp.zeros((1, C), F32)
    for f in range(2):

        def row_sums(r, carry):
            s, q = carry
            x = lat[f, r].astype(F32)
            return s + x, q + x * x

        zero = jnp.zeros((COLS, C), F32)
        s, q = lax.fori_loop(0, ROWS, row_sums, (zero, zero))
        total = total + valid[f] * jnp.sum(s, axis=0, keepdims=True)
        squares = squares + valid[f] * jnp.sum(q, axis=0, keepdims=True)
    chan, lane = iota((C, 128), 0), iota((C, 128), 1)
    to_sum = jnp.where(chan // CG == lane, 1.0, 0.0).astype(F32)
    to_square = jnp.where(chan // CG + GROUPS == lane, 1.0, 0.0).astype(F32)
    packed = exact_dot(jnp.broadcast_to(total, (8, C)), to_sum) + exact_dot(
        jnp.broadcast_to(squares, (8, C)), to_square
    )
    stat[...] = packed[0:1]

    sub = iota((8, C), 0)

    def edge_rows(f, e, p):
        if e < 2:
            return lat[f, 0 if e == 0 else ROWS - 1, 8 * p : 8 * p + 8].astype(F32)
        found = jnp.zeros((8, C), F32)
        for q in range(8):
            if e == 2:
                block = lat[f, 8 * p + q, 0:16].astype(F32)[0:8]
                turned = pltpu.roll(block, q, 0) if q else block
            else:
                block = lat[f, 8 * p + q, 16:32].astype(F32)[8:16]
                turned = pltpu.roll(block, q + 1, 0) if q < 7 else block
            found = jnp.where(sub == q, turned, found)
        return found

    def quads(x, y):
        turned = pltpu.roll(x, 4, 0), pltpu.roll(y, 4, 0)
        top = sub[:, :128] < 4
        return jnp.where(top, x, turned[1]), jnp.where(top, turned[0], y)

    def lanes(x):
        return [x[:, 128 * q : 128 * (q + 1)] for q in range(4)]

    for f in range(2):
        for e in range(4):
            for p in range(4):
                q = lanes(edge_rows(f, e, p))
                front, back = quads(q[0], q[1]), quads(q[2], q[3])
                for i in range(2):
                    send1[f, e * 8 + 2 * p + i] = jnp.concatenate(
                        [front[i], back[i]], axis=0
                    ).astype(BF16)

    pl.semaphore_wait(barrier, N - 1)

    to_all(by_distance, lambda to: send(0, stat, srecv, to))
    to_all(by_distance, lambda to: send(1, send1.at[0, to], recv1.at[0], to))
    to_all(by_distance, lambda to: send(2, send1.at[1, to], recv1.at[1], to))
    srecv[me] = stat[...]
    for f in range(2):
        recv1[f, me] = send1[f, me]

    kind = me // 8
    part = lax.rem(me, 8)
    tos_row = tos_v[...].astype(F32)
    owner = iota((N * 8, N), 0) // 8
    tile_here = jnp.sum(
        jnp.where(owner == iota((N * 8, N), 1), jnp.broadcast_to(tos_row, (N * 8, N)), 0.0),
        axis=1, keepdims=True,
    ).astype(jnp.int32)
    expand = jnp.where(
        iota((N, N * 8), 0) == lax.rem(iota((N, N * 8), 1) // 4, N), 1.0, 0.0
    ).astype(F32)
    tile_there = exact_dot(jnp.broadcast_to(tos_row, (8, N)), expand)[0:1].astype(jnp.int32)
    row_step = jnp.where(kind == 0, 1, jnp.where(kind == 1, -1, 0))
    col_step = jnp.where(kind == 2, 1, jnp.where(kind == 3, -1, 0))
    line8 = lax.rem(iota((N * 8, 1), 0), 8)
    turn = jnp.where(kind < 2, 1, 100)
    low_end = jnp.where((line8 == 4) & (part == 0), turn, 0)
    high_end = jnp.where((line8 == 7) & (part == 7), turn, 0)
    near_row = lax.rem(tile_here, PER_VIDEO) // TX + row_step
    near_col = lax.rem(tile_here, TX) + col_step + low_end - high_end
    inside = (near_row >= 0) & (near_row < TY) & (near_col >= 0) & (near_col < TX)
    near = jnp.where(
        inside, tile_here // PER_VIDEO * PER_VIDEO + near_row * TX + near_col, -1
    )
    there = iota((N * 8, N * 8), 1)
    same_line = lax.rem(iota((N * 8, N * 8), 0), 8) == there // (4 * N) * 4 + lax.rem(there, 4)
    pick[...] = jnp.where((near == tile_there) & same_line, 1.0, 0.0).astype(BF16)

    w_copy.wait()

    def add_weights(i, carry):
        tap, at = i // 4, pl.multiple_of(lax.rem(i, 4) * 128, 128)
        rows = pl.ds(at, 128)
        whole_sum = (
            w[tap, rows].astype(F32) + w[9 + tap, rows].astype(F32) + w[18 + tap, rows].astype(F32)
        )
        wa[tap, rows] = whole_sum.astype(BF16)
        return carry

    lax.fori_loop(0, 36, add_weights, 0)
    for u in range(2):
        hp[u, 0] = jnp.zeros((COLS, C), BF16)
        hp[u, ROWS + 1] = jnp.zeros((COLS, C), BF16)

    whole(0, srecv).wait_recv()
    sums = [jnp.zeros((1, 128), F32), jnp.zeros((1, 128), F32)]
    for s in range(N):
        row = srecv[s]
        second = jnp.where(tos_s[s] >= PER_VIDEO, 1.0, 0.0).astype(F32)
        sums = [sums[0] + row * (1.0 - second), sums[1] + row * second]
    lane, chan = iota((128, C), 0), iota((128, C), 1)
    from_sum = jnp.where(chan // CG == lane, 1.0, 0.0).astype(F32)
    from_square = jnp.where(chan // CG + GROUPS == lane, 1.0, 0.0).astype(F32)
    shift8 = jnp.broadcast_to(shift_ref[...], (8, C))

    def fold(x):
        q = lanes(x)
        top = sub[:, :128] < 4
        return jnp.concatenate([jnp.where(top, q[0], q[1]), jnp.where(top, q[2], q[3])], axis=0)

    for v in range(2):
        count = len_s[v].astype(F32) * COUNT
        spread = jnp.broadcast_to(sums[v], (8, 128))
        mean = exact_dot(spread, from_sum) / count
        square = exact_dot(spread, from_square) / count
        scale = (1.0 / jnp.sqrt(square - mean * mean + 1e-06)) * gain_ref[...]
        norm[v, 0] = mean
        norm[v, 1] = scale
        norm16[v, 0] = fold(mean)
        norm16[v, 1] = fold(scale)

    mine = jnp.where(my_second, 1, 0)
    mean = jnp.concatenate([norm[mine, 0]] * 4, axis=0)
    scale = jnp.concatenate([norm[mine, 1]] * 4, axis=0)
    shift = jnp.concatenate([shift8] * 4, axis=0)

    def hidden_row(r, carry):
        first = activate(lat[0, r].astype(F32), mean, scale, shift)
        second = activate(lat[1, r].astype(F32), mean, scale, shift)
        hp[0, r + 1] = first.astype(BF16)
        hp[1, r + 1] = (second - first).astype(BF16)
        return carry

    lax.fori_loop(0, ROWS, hidden_row, 0)
    col = lax.rem(iota((CHUNK * COLS, CO), 0), COLS)

    def conv_rows(u, r0):
        parts = []
        for c in range(3):
            part_sum = None
            for b in range(3):
                window = hp[u, pl.ds(r0 + b, CHUNK)].reshape(CHUNK * COLS, C)
                weight = wa[3 * b + c] if u == 0 else w[18 + 3 * b + c]
                product = dot(window, weight)
                part_sum = product if part_sum is None else part_sum + product
            parts.append(part_sum)
        result = (
            parts[1]
            + jnp.where(col > 0, pltpu.roll(parts[0], 1, 0), 0.0)
            + jnp.where(col < COLS - 1, pltpu.roll(parts[2], CHUNK * COLS - 1, 0), 0.0)
        )
        acc[u, pl.ds(r0, CHUNK)] = result.reshape(CHUNK, COLS, CO)

    steps = [(u, r0) for u in range(2) for r0 in range(0, ROWS, CHUNK)]
    for step in steps[:EARLY]:
        conv_rows(*step)

    shift16 = fold(shift8)
    base = jnp.where(kind == 0, 6, jnp.where(kind == 2, 2, 0))
    stride = jnp.where(kind < 2, 1, 3)
    px = lax.rem(iota((N * 4, CO), 0), 4)

    def second_send(u, to):
        send(3 + u, send2.at[u, to], recv2.at[u], to)

    for u in range(2):
        whole(1 + u, recv1.at[u]).wait_recv()

        def chunk_rows(i, carry):
            rows = []
            for j in range(2):
                pair = []
                for k in range(2):
                    s = 4 * i + 2 * j + k
                    v = jnp.where(tos_s[s] >= PER_VIDEO, 1, 0)
                    pair.append(
                        activate(recv1[u, s].astype(F32), norm16[v, 0], norm16[v, 1], shift16)
                    )
                front = quads(pair[0][:8], pair[1][:8])
                back = quads(pair[0][8:], pair[1][8:])
                rows.append(jnp.concatenate([*front, *back], axis=1))
            at = pl.ds(pl.multiple_of(16 * i, 16), 16)
            rows = jnp.concatenate(rows, axis=0)
            if u == 1:
                rows = rows - edge[0, at].astype(F32)
            edge[u, at] = rows.astype(BF16)
            return carry

        lax.fori_loop(0, N // 4, chunk_rows, 0, unroll=2)
        taps = []
        for t in range(3):
            tap = base + stride * t
            taps.append(dot(edge[u], wa[tap] if u == 0 else w[18 + tap]))
        main = (
            taps[1]
            + jnp.where(px >= 1, pltpu.roll(taps[0], 1, 0), 0.0)
            + jnp.where(px <= 2, pltpu.roll(taps[2], N * 4 - 1, 0), 0.0)
        )
        extra = jnp.where(px == 3, taps[0], jnp.where(px == 0, taps[2], 0.0))
        both = jnp.concatenate([main, extra], axis=0).astype(BF16)
        picked = dot(pick[...], both).reshape(N, 8, CO)
        send2[u] = jnp.concatenate([picked[..., :128], picked[..., 128:]], axis=1).astype(BF16)
        to_all((0,), functools.partial(second_send, u), (0, 8, 16, 24))
        recv2[u, me] = send2[u, me]

    for u in range(2):
        to_all((1, 2, 3), functools.partial(second_send, u), (0, 8, 16, 24))

    for step in steps[EARLY:]:
        conv_rows(*step)

    for u in range(2):
        whole(3 + u, recv2.at[u]).wait_recv()

    def hits(shape, half, pos):
        at = iota(shape, 1)
        g, r = at // 16, lax.rem(at, 8)
        lands = jnp.where(
            r < 4,
            4 * g + r,
            jnp.where(
                r == 4,
                lax.rem(4 * g + 31, 32),
                jnp.where(r == 7, lax.rem(4 * g + 4, 32), -1),
            ),
        )
        return (lax.rem(at, 16) // 8 == half) & (lands == pos)

    def arrived(e):
        both = [recv2[u, 8 * e : 8 * e + 8].reshape(128, 128) for u in range(2)]
        return jnp.concatenate(both, axis=1)

    line_at = iota((64, 128), 0)
    to_line = jnp.where(hits((64, 128), line_at // 32, lax.rem(line_at, 32)), 1.0, 0.0).astype(BF16)
    for e, row in ((0, ROWS - 1), (1, 0)):
        line = dot(to_line, arrived(e))
        for u in range(2):
            for half in range(2):
                acc[u, row, :, 128 * half : 128 * half + 128] += line[
                    32 * half : 32 * half + 32, 128 * u : 128 * u + 128
                ]
    side_at = iota((512, 128), 0)
    on_side = hits((512, 128), side_at // 256, lax.rem(side_at, 256) // 8)
    for e, at in ((2, COLS - 8), (3, 0)):
        to_side = jnp.where(on_side & (lax.rem(side_at, 8) == (7 if e == 2 else 0)), 1.0, 0.0)
        side = dot(to_side.astype(BF16), arrived(e)).reshape(2, ROWS, 8, CO)
        for u in range(2):
            for half in range(2):
                acc[u, :, at : at + 8, 128 * half : 128 * half + 128] += side[
                    half, :, :, 128 * u : 128 * u + 128
                ]

    bias = jnp.broadcast_to(bias_ref[...], (COLS, CO))

    def finish(r, carry):
        first = acc[0, r] + bias
        out_ref[0, r] = (first * valid[0]).astype(BF16)
        out_ref[1, r] = ((first + acc[1, r]) * valid[1]).astype(BF16)
        return carry

    lax.fori_loop(0, ROWS, finish, 0)
    whole(0, srecv).wait_send()
    for u in range(2):
        whole(1 + u, recv1.at[u]).wait_send()
        whole(3 + u, recv2.at[u]).wait_send()


def body(latent, lengths, tile_of_slot, norm_gain, norm_shift, conv_weight, conv_bias):
    vmem = pl.BlockSpec(memory_space=pltpu.VMEM)
    hbm = pl.BlockSpec(memory_space=pltpu.HBM)
    decoded = pl.pallas_call(
        kernel,
        out_shape=jax.ShapeDtypeStruct((2, ROWS, COLS, CO), BF16),
        in_specs=[hbm] * 8,
        out_specs=vmem,
        scratch_shapes=[
            pltpu.VMEM((2, ROWS, COLS, C), BF16),
            pltpu.VMEM((27, C, CO), BF16),
            pltpu.VMEM((9, C, CO), BF16),
            pltpu.VMEM((2, ROWS + 2, COLS, C), BF16),
            pltpu.VMEM((2, ROWS, COLS, CO), F32),
            pltpu.VMEM((2, N, 16, 128), BF16),
            pltpu.VMEM((2, N, 16, 128), BF16),
            pltpu.VMEM((2, N, 16, 128), BF16),
            pltpu.VMEM((2, N, 16, 128), BF16),
            pltpu.VMEM((1, 128), F32),
            pltpu.VMEM((N, 1, 128), F32),
            pltpu.VMEM((2, 2, 8, C), F32),
            pltpu.VMEM((2, 2, 16, 128), F32),
            pltpu.VMEM((2, N * 4, C), BF16),
            pltpu.VMEM((N * 8, N * 8), BF16),
            pltpu.SMEM((N,), jnp.int32),
            pltpu.SMEM((2,), jnp.int32),
            pltpu.VMEM((1, N), jnp.int32),
            pltpu.VMEM((1, C), F32),
            pltpu.VMEM((1, C), F32),
            pltpu.VMEM((1, CO), F32),
            pltpu.SemaphoreType.DMA(()),
            pltpu.SemaphoreType.DMA(()),
            pltpu.SemaphoreType.DMA((6,)),
            pltpu.SemaphoreType.DMA((5,)),
            pltpu.SemaphoreType.DMA((5,)),
        ],
        compiler_params=pltpu.CompilerParams(
            collective_id=0, has_side_effects=True, vmem_limit_bytes=40 << 20
        ),
    )(
        *(
            pltpu.with_memory_space_constraint(x, pltpu.HBM)
            for x in (
                latent[0],
                conv_weight.reshape(27, C, CO),
                tile_of_slot,
                lengths,
                tile_of_slot.reshape(1, N),
                norm_gain.reshape(1, C),
                norm_shift.reshape(1, C),
                conv_bias.reshape(1, CO),
            )
        )
    )
    return decoded[None]


def solution(mesh):
    placed = (P(("grp", "tile"), None, None, None, None), P("grp"), P("grp"), P(), P(), P(), P())
    return jax.shard_map(
        body,
        mesh=mesh,
        in_specs=placed,
        out_specs=P(("grp", "tile"), None, None, None, None),
        check_vma=False,
    )
```

time: 37.6 us -> 29.8 us (0.79)
  local copies, waits for them, and re-layouts: 5.91 us -> 0.97 us
  Pallas kernels: 31.5 us -> 28.5 us
    unnamed x13 -> x1, local copies, waits for them, and re-layouts: 5.91 us -> 0.97 us
    pallas_call x1, Pallas kernels: 31.5 us -> 28.5 us  [body(): pl.pallas_call(kernel, out_shape=jax.ShapeDtypeStruct((2, ROWS, COLS, CO)...]
where the time goes in v2:
time: 29.8 us; the launch traced here: 29.5 us
  Pallas kernels  28.5 us (96%)
  local copies, waits for them, and re-layouts  0.97 us (3%)
    pallas_call x1, Pallas kernels, body(): pl.pallas_call(kernel, out_shape=jax.ShapeDtypeStruct((2, ROWS, COLS, CO)...  28.5 us
    unnamed x1, local copies, waits for them, and re-layouts  0.97 us

profile of v2, /device:TPU:1, one launch (start us, length us, event | category | flops | bytes accessed | tf_op | source)
XLA Modules:
  0.0 29.5 jit_solution(12015907189510076036)
XLA Ops:
  0.0 28.5 %shard_map.73 = bf16[2,32,32,256]{3,2,1,0:T(8,128)(2,1)S(1)} custom-call(bf16[2,32,32,512]{3,2,1,0:T(8,128)(2,1)} %bitcast.9, bf16[27,512,256]{2,1,0:T(8,128)(2,1)} %bitcast.8, s32[32]{0:T(128)} %tos_hbm.1, s32[2]{0:T(128)} %len_hbm.1, s32[1,32]{1,0:T(1,128)} %bitcast.10, f32[1,512]{1,0:T(1,128)} %bitcast.11, f32[1,512]{1,0:T(1,128)} %bitcast.12, ...), custom_call_target="tpu_custom_call" | custom-call | tf_op jit(solution)/shard_map/pallas_call | solution.py:396
  28.6 1.0 %copy.9 = bf16[1,2,32,32,256]{4,3,2,1,0:T(8,128)(2,1)} copy(bf16[1,2,32,32,256]{4,3,2,1,0:T(8,128)(2,1)S(1)} %bitcast.7) | data formatting | bytes 2097152

commit v3 on v2

v3 whole, which is shorter than its diff:
```python
import functools

import jax
import jax.numpy as jnp
from jax import lax
from jax.experimental import pallas as pl
from jax.experimental.pallas import tpu as pltpu
from jax.sharding import PartitionSpec as P

MESH = pl.DeviceIdType.MESH
F32 = jnp.float32
BF16 = jnp.bfloat16
GROUPS = 32
N = 32
ROWS = 32
COLS = 32
C = 512
CO = 256
CG = C // GROUPS
PER_VIDEO = 16
TX = 4
TY = 4
COUNT = float(TY * ROWS * TX * COLS * CG)
CHUNK = 16
EARLY = 0


def iota(shape, dim):
    return lax.broadcasted_iota(jnp.int32, shape, dim)


def thirds(x):
    high = x.astype(BF16).astype(F32)
    rest = x - high
    middle = rest.astype(BF16).astype(F32)
    return high, middle, rest - middle


def one_hot(mask):
    return jnp.where(mask, 1.0, 0.0).astype(BF16)


def dot(a, b):
    return jnp.dot(a, b, preferred_element_type=F32)


def activate(x, scale, offset):
    half = x * scale + offset
    return (half + half * jnp.tanh(half)).astype(BF16).astype(F32)


def kernel(
    lat_hbm, w_hbm, tos_hbm, len_hbm, tos_row_hbm, gain_hbm, shift_hbm, bias_hbm, out_ref,
    lat, w, wc, hp, acc, send1, recv1, send2, recv2, stat, srecv, norm, norm16, edge, pick, to_line, to_side,
    tos_s, len_s, tos_v, gain_ref, shift_ref, bias_ref,
    lat_sem, w_sem, small_sem, ssem, rsem,
):
    me = lax.axis_index("tile")
    grp = lax.axis_index("grp")
    my_x, my_z, my_core = me // 8, lax.rem(me // 2, 4), lax.rem(me, 2)

    def to_all(planes, action, fixed=False):
        xs = [8 * j if fixed else lax.rem(my_x + 2 + j, 4) * 8 for j in range(4)]
        for plane in planes:
            for x in xs:
                for core in (my_core, 1 - my_core):
                    to = x + plane * 2 + core
                    pl.when(to != me)(functools.partial(action, to))

    by_distance = (
        lax.rem(my_z + 2, 4), 3 - my_z, my_z + 1 - 2 * lax.rem(my_z, 2), my_z
    )
    barrier = pltpu.get_barrier_semaphore()

    def greet(to):
        pl.semaphore_signal(barrier, inc=1, device_id=(grp, to), device_id_type=MESH)

    to_all((by_distance[1], by_distance[0], by_distance[2], by_distance[3]), greet)
    lat_copies = [pltpu.make_async_copy(lat_hbm.at[f], lat.at[f], lat_sem.at[f]) for f in range(2)]
    for copy in lat_copies:
        copy.start()
    early_copy = pltpu.make_async_copy(w_hbm.at[0:18], w, w_sem.at[0])
    last_copy = pltpu.make_async_copy(w_hbm.at[18:27], wc.at[1], w_sem.at[1])

    small = [
        pltpu.make_async_copy(src, dst, small_sem.at[i])
        for i, (src, dst) in enumerate(
            (
                (tos_hbm, tos_s), (len_hbm, len_s), (tos_row_hbm, tos_v),
                (gain_hbm, gain_ref), (shift_hbm, shift_ref), (bias_hbm, bias_ref),
            )
        )
    ]
    for copy in small:
        copy.start()

    def send(phase, src, dst, to, slot=None):
        pltpu.make_async_remote_copy(
            src_ref=src, dst_ref=dst.at[me] if slot is None else dst.at[me, slot], send_sem=ssem.at[phase], recv_sem=rsem.at[phase],
            device_id=(grp, to), device_id_type=MESH,
        ).start()

    def whole(phase, dst):
        part = dst.at[pl.ds(0, N - 1)]
        return pltpu.make_async_remote_copy(
            src_ref=part, dst_ref=part, send_sem=ssem.at[phase], recv_sem=rsem.at[phase],
            device_id=(grp, lax.rem(me + 1, N)), device_id_type=MESH,
        )

    for copy in small:
        copy.wait()
    my_tile = tos_s[me]
    my_second = my_tile >= PER_VIDEO
    my_length = jnp.where(my_second, len_s[1], len_s[0])
    valid = [jnp.where(my_length > f, 1.0, 0.0).astype(F32) for f in range(2)]

    by_group = one_hot((iota((C, 128), 0) >> 4) == iota((C, 128), 1))
    total = jnp.zeros((1, C), F32)
    squares = jnp.zeros((1, C), F32)
    for f in range(2):
        lat_copies[f].wait()

        def row_sums(r, carry):
            s, q = carry
            x = lat[f, r].astype(F32)
            return s + x, q + x * x

        zero = jnp.zeros((COLS, C), F32)
        s, q = lax.fori_loop(0, ROWS, row_sums, (zero, zero))
        total = total + valid[f] * jnp.sum(s, axis=0, keepdims=True)
        squares = squares + valid[f] * jnp.sum(q, axis=0, keepdims=True)
    sub = iota((8, C), 0)
    early_copy.start()
    last_copy.start()
    six = jnp.zeros((8, C), F32)
    for i, row in enumerate((*thirds(total), *thirds(squares))):
        six = jnp.where(sub == i, jnp.broadcast_to(row, (8, C)), six)
    packed = dot(six.astype(BF16), by_group)
    stat[...] = packed[0:1] + packed[1:2] + packed[2:3] + pltpu.roll(
        packed[3:4] + packed[4:5] + packed[5:6], GROUPS, 1
    )

    def edge_rows(f, e, p):
        if e < 2:
            return lat[f, 0 if e == 0 else ROWS - 1, 8 * p : 8 * p + 8].astype(F32)
        found = jnp.zeros((8, C), F32)
        for q in range(8):
            if e == 2:
                block = lat[f, 8 * p + q, 0:16].astype(F32)[0:8]
                turned = pltpu.roll(block, q, 0) if q else block
            else:
                block = lat[f, 8 * p + q, 16:32].astype(F32)[8:16]
                turned = pltpu.roll(block, q + 1, 0) if q < 7 else block
            found = jnp.where(sub == q, turned, found)
        return found

    def quads(x, y):
        turned = pltpu.roll(x, 4, 0), pltpu.roll(y, 4, 0)
        top = sub[:, :128] < 4
        return jnp.where(top, x, turned[1]), jnp.where(top, turned[0], y)

    def lanes(x):
        return [x[:, 128 * q : 128 * (q + 1)] for q in range(4)]

    for f in range(2):
        for e in range(4):
            for p in range(4):
                q = lanes(edge_rows(f, e, p))
                front, back = quads(q[0], q[1]), quads(q[2], q[3])
                for i in range(2):
                    send1[f, e * 8 + 2 * p + i] = jnp.concatenate(
                        [front[i], back[i]], axis=0
                    ).astype(BF16)

    pl.semaphore_wait(barrier, N - 1)

    to_all(by_distance, lambda to: send(0, stat, srecv, to))
    to_all(by_distance, lambda to: send(1, send1.at[0, to], recv1.at[0], to))
    to_all(by_distance, lambda to: send(2, send1.at[1, to], recv1.at[1], to))
    srecv[me] = stat[...]
    for f in range(2):
        recv1[f, me] = send1[f, me]

    kind = me // 8
    part = lax.rem(me, 8)
    tos_row = tos_v[...].astype(F32)
    owner = iota((N * 8, N), 0) >> 3
    tile_here = jnp.sum(
        jnp.where(owner == iota((N * 8, N), 1), jnp.broadcast_to(tos_row, (N * 8, N)), 0.0),
        axis=1, keepdims=True,
    ).astype(jnp.int32)
    expand = one_hot(iota((N, N * 8), 0) == (iota((N, N * 8), 1) >> 2) & (N - 1))
    tile_there = dot(jnp.broadcast_to(tos_row, (8, N)).astype(BF16), expand)[0:1].astype(jnp.int32)
    row_step = jnp.where(kind == 0, 1, jnp.where(kind == 1, -1, 0))
    col_step = jnp.where(kind == 2, 1, jnp.where(kind == 3, -1, 0))
    line8 = iota((N * 8, 1), 0) & 7
    turn = jnp.where(kind < 2, 1, 100)
    low_end = jnp.where((line8 == 4) & (part == 0), turn, 0)
    high_end = jnp.where((line8 == 7) & (part == 7), turn, 0)
    near_row = ((tile_here & (PER_VIDEO - 1)) >> 2) + row_step
    near_col = (tile_here & (TX - 1)) + col_step + low_end - high_end
    inside = (near_row >= 0) & (near_row < TY) & (near_col >= 0) & (near_col < TX)
    near = jnp.where(
        inside, (tile_here & PER_VIDEO) + near_row * TX + near_col, -1
    )
    there = iota((N * 8, N * 8), 1)
    same_line = (iota((N * 8, N * 8), 0) & 7) == ((there >> 7) << 2) + (there & 3)
    pick[...] = jnp.where((near == tile_there) & same_line, 1.0, 0.0).astype(BF16)

    early_copy.wait()
    last_copy.wait()

    def add_weights(i, carry):
        tap, at = i // 4, pl.multiple_of(lax.rem(i, 4) * 128, 128)
        rows = pl.ds(at, 128)
        whole_sum = (
            w[tap, rows].astype(F32) + w[9 + tap, rows].astype(F32) + wc[1, tap, rows].astype(F32)
        )
        wc[0, tap, rows] = whole_sum.astype(BF16)
        return carry

    lax.fori_loop(0, 36, add_weights, 0)
    for u in range(2):
        hp[u, 0] = jnp.zeros((COLS, C), BF16)
        hp[u, ROWS + 1] = jnp.zeros((COLS, C), BF16)

    def hits(shape, half, pos):
        at = iota(shape, 1)
        g, r = at >> 4, at & 7
        lands = jnp.where(
            r < 4,
            4 * g + r,
            jnp.where(
                r == 4,
                (4 * g + 31) & 31,
                jnp.where(r == 7, (4 * g + 4) & 31, -1),
            ),
        )
        return (((at >> 3) & 1) == half) & (lands == pos)

    line_at = iota((64, 128), 0)
    to_line[...] = one_hot(hits((64, 128), line_at >> 5, line_at & 31))
    side_at = iota((512, 128), 0)
    on_side = hits((512, 128), side_at >> 8, (side_at & 255) >> 3)
    for i, edge_sub in enumerate((7, 0)):
        to_side[i] = one_hot(on_side & ((side_at & 7) == edge_sub))

    lane = iota((1, 128), 1)
    lane8, chan = iota((128, C), 0), iota((128, C), 1)
    to_channels = one_hot(((chan >> 4) == (lane8 & (GROUPS - 1))) & (lane8 < 3 * GROUPS))
    gain8 = jnp.broadcast_to(gain_ref[...] * 0.5, (8, C))
    shift8 = jnp.broadcast_to(shift_ref[...] * 0.5, (8, C))
    whole(0, srecv).wait_recv()
    sums = [jnp.zeros((1, 128), F32), jnp.zeros((1, 128), F32)]
    for s in range(N):
        row = srecv[s]
        second = jnp.where(tos_s[s] >= PER_VIDEO, 1.0, 0.0).astype(F32)
        sums = [sums[0] + row * (1.0 - second), sums[1] + row * second]
    four = jnp.zeros((8, 128), F32)
    for v in range(2):
        scaled = sums[v] / (len_s[v].astype(F32) * COUNT)
        mean = jnp.where(lane < GROUPS, scaled, 0.0)
        square = jnp.where(lane < GROUPS, pltpu.roll(scaled, 128 - GROUPS, 1), 0.0)
        inv = jnp.where(lane < GROUPS, 1.0 / jnp.sqrt(square - mean * mean + 1e-06), 0.0)
        for i, row in enumerate((mean, inv)):
            high, middle, low = thirds(row)
            row = high + pltpu.roll(middle, GROUPS, 1) + pltpu.roll(low, 2 * GROUPS, 1)
            four = jnp.where(sub[:, :128] == 2 * v + i, jnp.broadcast_to(row, (8, 128)), four)
    spread = dot(four.astype(BF16), to_channels)

    def fold(x):
        q = lanes(x)
        top = sub[:, :128] < 4
        return jnp.concatenate([jnp.where(top, q[0], q[1]), jnp.where(top, q[2], q[3])], axis=0)

    for v in range(2):
        mean = jnp.broadcast_to(spread[2 * v : 2 * v + 1], (8, C))
        scale = jnp.broadcast_to(spread[2 * v + 1 : 2 * v + 2], (8, C)) * gain8
        offset = shift8 - mean * scale
        norm[v, 0] = scale
        norm[v, 1] = offset
        norm16[v, 0] = fold(scale)
        norm16[v, 1] = fold(offset)

    mine = jnp.where(my_second, 1, 0)
    scale = jnp.concatenate([norm[mine, 0]] * 4, axis=0)
    offset = jnp.concatenate([norm[mine, 1]] * 4, axis=0)

    def hidden_row(r, carry):
        first = activate(lat[0, r].astype(F32), scale, offset)
        second = activate(lat[1, r].astype(F32), scale, offset)
        hp[0, r + 1] = first.astype(BF16)
        hp[1, r + 1] = (second - first).astype(BF16)
        return carry

    lax.fori_loop(0, ROWS, hidden_row, 0)
    col = iota((CHUNK * COLS, CO), 0) & (COLS - 1)

    def conv_rows(i, carry):
        per = ROWS // CHUNK
        u, r0 = lax.div(i, per), lax.rem(i, per) * CHUNK
        parts = []
        for c in range(3):
            part_sum = None
            for b in range(3):
                window = hp[u, pl.ds(r0 + b, CHUNK)].reshape(CHUNK * COLS, C)
                product = dot(window, wc[u, 3 * b + c])
                part_sum = product if part_sum is None else part_sum + product
            parts.append(part_sum)
        result = (
            parts[1]
            + jnp.where(col > 0, pltpu.roll(parts[0], 1, 0), 0.0)
            + jnp.where(col < COLS - 1, pltpu.roll(parts[2], CHUNK * COLS - 1, 0), 0.0)
        )
        acc[u, pl.ds(r0, CHUNK)] = result.reshape(CHUNK, COLS, CO)
        return carry

    if EARLY:
        lax.fori_loop(0, EARLY, conv_rows, 0)

    base = jnp.where(kind == 0, 6, jnp.where(kind == 2, 2, 0))
    stride = jnp.where(kind < 2, 1, 3)
    px = iota((N * 4, CO), 0) & 3

    for u in range(2):
        whole(1 + u, recv1.at[u]).wait_recv()

        def chunk_rows(i, carry):
            rows = []
            for j in range(2):
                pair = []
                for k in range(2):
                    s = 4 * i + 2 * j + k
                    v = jnp.where(tos_s[s] >= PER_VIDEO, 1, 0)
                    pair.append(
                        activate(recv1[u, s].astype(F32), norm16[v, 0], norm16[v, 1])
                    )
                front = quads(pair[0][:8], pair[1][:8])
                back = quads(pair[0][8:], pair[1][8:])
                rows.append(jnp.concatenate([*front, *back], axis=1))
            at = pl.ds(pl.multiple_of(16 * i, 16), 16)
            rows = jnp.concatenate(rows, axis=0)
            if u == 1:
                rows = rows - edge[0, at].astype(F32)
            edge[u, at] = rows.astype(BF16)
            return carry

        lax.fori_loop(0, N // 4, chunk_rows, 0, unroll=2)
        taps = []
        for t in range(3):
            tap = base + stride * t
            taps.append(dot(edge[u], wc[u, tap]))
        main = (
            taps[1]
            + jnp.where(px >= 1, pltpu.roll(taps[0], 1, 0), 0.0)
            + jnp.where(px <= 2, pltpu.roll(taps[2], N * 4 - 1, 0), 0.0)
        )
        extra = jnp.where(px == 3, taps[0], jnp.where(px == 0, taps[2], 0.0))
        both = jnp.concatenate([main, extra], axis=0).astype(BF16)
        picked = dot(pick[...], both).reshape(N, 8, CO)
        send2[:, u] = jnp.concatenate([picked[..., :128], picked[..., 128:]], axis=1).astype(BF16)
        to_all((0,), lambda to: send(3, send2.at[to, u], recv2, to, u), True)
        recv2[me, u] = send2[me, u]

    to_all((1, 2, 3), lambda to: send(3, send2.at[to], recv2, to), True)

    lax.fori_loop(EARLY, 2 * ROWS // CHUNK, conv_rows, 0)

    whole(3, recv2).wait_recv()

    def arrived(e):
        both = [recv2[8 * e : 8 * e + 8, u].reshape(128, 128) for u in range(2)]
        return jnp.concatenate(both, axis=1)

    for e, row in ((0, ROWS - 1), (1, 0)):
        line = dot(to_line[...], arrived(e))
        for u in range(2):
            for half in range(2):
                acc[u, row, :, 128 * half : 128 * half + 128] += line[
                    32 * half : 32 * half + 32, 128 * u : 128 * u + 128
                ]
    for e, at in ((2, COLS - 8), (3, 0)):
        side = dot(to_side[e - 2], arrived(e)).reshape(2, ROWS, 8, CO)
        for u in range(2):
            for half in range(2):
                acc[u, :, at : at + 8, 128 * half : 128 * half + 128] += side[
                    half, :, :, 128 * u : 128 * u + 128
                ]

    bias = jnp.broadcast_to(bias_ref[...], (COLS, CO))

    def finish(r, carry):
        first = acc[0, r] + bias
        out_ref[0, r] = (first * valid[0]).astype(BF16)
        out_ref[1, r] = ((first + acc[1, r]) * valid[1]).astype(BF16)
        return carry

    lax.fori_loop(0, ROWS, finish, 0)
    whole(0, srecv).wait_send()
    whole(3, recv2).wait_send()
    for u in range(2):
        whole(1 + u, recv1.at[u]).wait_send()


def body(latent, lengths, tile_of_slot, norm_gain, norm_shift, conv_weight, conv_bias):
    vmem = pl.BlockSpec(memory_space=pltpu.VMEM)
    hbm = pl.BlockSpec(memory_space=pltpu.HBM)
    decoded = pl.pallas_call(
        kernel,
        out_shape=jax.ShapeDtypeStruct((2, ROWS, COLS, CO), BF16),
        in_specs=[hbm] * 8,
        out_specs=vmem,
        scratch_shapes=[
            pltpu.VMEM((2, ROWS, COLS, C), BF16),
            pltpu.VMEM((18, C, CO), BF16),
            pltpu.VMEM((2, 9, C, CO), BF16),
            pltpu.VMEM((2, ROWS + 2, COLS, C), BF16),
            pltpu.VMEM((2, ROWS, COLS, CO), F32),
            pltpu.VMEM((2, N, 16, 128), BF16),
            pltpu.VMEM((2, N, 16, 128), BF16),
            pltpu.VMEM((N, 2, 16, 128), BF16),
            pltpu.VMEM((N, 2, 16, 128), BF16),
            pltpu.VMEM((1, 128), F32),
            pltpu.VMEM((N, 1, 128), F32),
            pltpu.VMEM((2, 2, 8, C), F32),
            pltpu.VMEM((2, 2, 16, 128), F32),
            pltpu.VMEM((2, N * 4, C), BF16),
            pltpu.VMEM((N * 8, N * 8), BF16),
            pltpu.VMEM((64, 128), BF16),
            pltpu.VMEM((2, 512, 128), BF16),
            pltpu.SMEM((N,), jnp.int32),
            pltpu.SMEM((2,), jnp.int32),
            pltpu.VMEM((1, N), jnp.int32),
            pltpu.VMEM((1, C), F32),
            pltpu.VMEM((1, C), F32),
            pltpu.VMEM((1, CO), F32),
            pltpu.SemaphoreType.DMA((2,)),
            pltpu.SemaphoreType.DMA((2,)),
            pltpu.SemaphoreType.DMA((6,)),
            pltpu.SemaphoreType.DMA((4,)),
            pltpu.SemaphoreType.DMA((4,)),
        ],
        compiler_params=pltpu.CompilerParams(
            collective_id=0, has_side_effects=True, vmem_limit_bytes=40 << 20
        ),
    )(
        *(
            pltpu.with_memory_space_constraint(x, pltpu.HBM)
            for x in (
                latent[0],
                conv_weight.reshape(27, C, CO),
                tile_of_slot,
                lengths,
                tile_of_slot.reshape(1, N),
                norm_gain.reshape(1, C),
                norm_shift.reshape(1, C),
                conv_bias.reshape(1, CO),
            )
        )
    )
    return decoded[None]


def solution(mesh):
    placed = (P(("grp", "tile"), None, None, None, None), P("grp"), P("grp"), P(), P(), P(), P())
    return jax.shard_map(
        body,
        mesh=mesh,
        in_specs=placed,
        out_specs=P(("grp", "tile"), None, None, None, None),
        check_vma=False,
    )
```

time: 29.8 us -> 28.9 us (0.970)
  Pallas kernels: 28.5 us -> 27.6 us
    pallas_call x1, Pallas kernels: 28.5 us -> 27.6 us  [body(): pl.pallas_call(kernel, out_shape=jax.ShapeDtypeStruct((2, ROWS, COLS, CO)...]
where the time goes in v3:
time: 28.9 us; the launch traced here: 28.6 us
  Pallas kernels  27.6 us (96%)
  local copies, waits for them, and re-layouts  0.97 us (3%)
    pallas_call x1, Pallas kernels, body(): pl.pallas_call(kernel, out_shape=jax.ShapeDtypeStruct((2, ROWS, COLS, CO)...  27.6 us
    unnamed x1, local copies, waits for them, and re-layouts  0.97 us

profile of v3, /device:TPU:1, one launch (start us, length us, event | category | flops | bytes accessed | tf_op | source)
XLA Modules:
  0.0 28.6 jit_solution(9400189698934314571)
XLA Ops:
  0.0 27.6 %shard_map.73 = bf16[2,32,32,256]{3,2,1,0:T(8,128)(2,1)S(1)} custom-call(bf16[2,32,32,512]{3,2,1,0:T(8,128)(2,1)} %bitcast.9, bf16[27,512,256]{2,1,0:T(8,128)(2,1)} %bitcast.8, s32[32]{0:T(128)} %tos_hbm.1, s32[2]{0:T(128)} %len_hbm.1, s32[1,32]{1,0:T(1,128)} %bitcast.10, f32[1,512]{1,0:T(1,128)} %bitcast.11, f32[1,512]{1,0:T(1,128)} %bitcast.12, ...), custom_call_target="tpu_custom_call" | custom-call | tf_op jit(solution)/shard_map/pallas_call | solution.py:408
  27.6 1.0 %copy.9 = bf16[1,2,32,32,256]{4,3,2,1,0:T(8,128)(2,1)} copy(bf16[1,2,32,32,256]{4,3,2,1,0:T(8,128)(2,1)S(1)} %bitcast.7) | data formatting | bytes 2097152

commit v4 on v3

--- a/solution.py
+++ b/solution.py
@@ -366,6 +366,23 @@
 
     lax.fori_loop(EARLY, 2 * ROWS // CHUNK, conv_rows, 0)
 
+    def finish_part(r, at, count):
+        cols = pl.ds(at, count)
+        first = acc[0, r, cols] + bias_ref[...]
+        out_ref[0, r, cols] = (first * valid[0]).astype(BF16)
+        out_ref[1, r, cols] = ((first + acc[1, r, cols]) * valid[1]).astype(BF16)
+
+    def finish(r, carry):
+        finish_part(r, 0, COLS)
+        return carry
+
+    def finish_sides(r, carry):
+        finish_part(r, 0, 8)
+        finish_part(r, COLS - 8, 8)
+        return carry
+
+    lax.fori_loop(0, ROWS, finish, 0)
+
     whole(3, recv2).wait_recv()
 
     def arrived(e):
@@ -387,15 +404,9 @@
                     half, :, :, 128 * u : 128 * u + 128
                 ]
 
-    bias = jnp.broadcast_to(bias_ref[...], (COLS, CO))
-
-    def finish(r, carry):
-        first = acc[0, r] + bias
-        out_ref[0, r] = (first * valid[0]).astype(BF16)
-        out_ref[1, r] = ((first + acc[1, r]) * valid[1]).astype(BF16)
-        return carry
-
-    lax.fori_loop(0, ROWS, finish, 0)
+    lax.fori_loop(0, ROWS, finish_sides, 0)
+    finish(0, 0)
+    finish(ROWS - 1, 0)
     whole(0, srecv).wait_send()
     whole(3, recv2).wait_send()
     for u in range(2):

time: 28.9 us -> 28.8 us (level)
  no operation moved by 1% of the time
where the time goes in v4:
time: 28.8 us; the launch traced here: 28.5 us
  Pallas kernels  27.5 us (95%)
  local copies, waits for them, and re-layouts  0.97 us (3%)
    pallas_call x1, Pallas kernels, body(): pl.pallas_call(kernel, out_shape=jax.ShapeDtypeStruct((2, ROWS, COLS, CO)...  27.5 us
    unnamed x1, local copies, waits for them, and re-layouts  0.97 us

profile of v4, /device:TPU:1, one launch (start us, length us, event | category | flops | bytes accessed | tf_op | source)
XLA Modules:
  0.0 28.5 jit_solution(3281718314320002370)
XLA Ops:
  0.0 27.5 %shard_map.73 = bf16[2,32,32,256]{3,2,1,0:T(8,128)(2,1)S(1)} custom-call(bf16[2,32,32,512]{3,2,1,0:T(8,128)(2,1)} %bitcast.9, bf16[27,512,256]{2,1,0:T(8,128)(2,1)} %bitcast.8, s32[32]{0:T(128)} %tos_hbm.1, s32[2]{0:T(128)} %len_hbm.1, s32[1,32]{1,0:T(1,128)} %bitcast.10, f32[1,512]{1,0:T(1,128)} %bitcast.11, f32[1,512]{1,0:T(1,128)} %bitcast.12, ...), custom_call_target="tpu_custom_call" | custom-call | tf_op jit(solution)/shard_map/pallas_call | solution.py:419
  27.5 1.0 %copy.9 = bf16[1,2,32,32,256]{4,3,2,1,0:T(8,128)(2,1)} copy(bf16[1,2,32,32,256]{4,3,2,1,0:T(8,128)(2,1)S(1)} %bitcast.7) | data formatting | bytes 2097152

commit v5 on v4

--- a/solution.py
+++ b/solution.py
@@ -21,7 +21,7 @@
 TX = 4
 TY = 4
 COUNT = float(TY * ROWS * TX * COLS * CG)
-CHUNK = 16
+CHUNK = 32
 EARLY = 0
 
 

time: 28.8 us -> 28.8 us (level)
  no operation moved by 1% of the time
where the time goes in v5:
time: 28.8 us; the launch traced here: 28.5 us
  Pallas kernels  27.5 us (95%)
  local copies, waits for them, and re-layouts  0.97 us (3%)
    pallas_call x1, Pallas kernels, body(): pl.pallas_call(kernel, out_shape=jax.ShapeDtypeStruct((2, ROWS, COLS, CO)...  27.5 us
    unnamed x1, local copies, waits for them, and re-layouts  0.97 us

profile of v5, /device:TPU:1, one launch (start us, length us, event | category | flops | bytes accessed | tf_op | source)
XLA Modules:
  0.0 28.5 jit_solution(6524714573553555698)
XLA Ops:
  0.0 27.5 %shard_map.73 = bf16[2,32,32,256]{3,2,1,0:T(8,128)(2,1)S(1)} custom-call(bf16[2,32,32,512]{3,2,1,0:T(8,128)(2,1)} %bitcast.9, bf16[27,512,256]{2,1,0:T(8,128)(2,1)} %bitcast.8, s32[32]{0:T(128)} %tos_hbm.1, s32[2]{0:T(128)} %len_hbm.1, s32[1,32]{1,0:T(1,128)} %bitcast.10, f32[1,512]{1,0:T(1,128)} %bitcast.11, f32[1,512]{1,0:T(1,128)} %bitcast.12, ...), custom_call_target="tpu_custom_call" | custom-call | tf_op jit(solution)/shard_map/pallas_call | solution.py:419
  27.5 1.0 %copy.9 = bf16[1,2,32,32,256]{4,3,2,1,0:T(8,128)(2,1)} copy(bf16[1,2,32,32,256]{4,3,2,1,0:T(8,128)(2,1)S(1)} %bitcast.7) | data formatting | bytes 2097152
